TPU v7x, 512 devices: a whole 4x8x8 slice. The times are simulated.
512 devices in a mesh: vocab: 16 (over y, core), docs: 32 (over x, z).
Axes of the slice: x: 4, y: 8, z: 8, core: 2. Of those that a mesh axis runs over, the one named last changes fastest.
Arguments:
- counts: bfloat16 [65536, 4, 128], P(('vocab', 'docs')), may hold values from 0 to 2
- doc_owner: int32 [65536, 4], P(('vocab', 'docs')), may hold values from 0 to 511, all different within a row; in each aligned block of 128 rows (0 to 127, 128 to 255, ...) at most 2 rows name the same one
- doc_sub: int32 [65536, 4], P(('vocab', 'docs')), may hold values from 0 to 7
- doc_len: int32 [65536], P(('vocab', 'docs')), may hold values from 256 to 1023
- first_weight: bfloat16 [524288, 2048], P(('vocab', 'docs')), may hold values from -0.25 to 0.25
- first_bias: float32 [2048], replicated, may hold values from -3 to 3
- head_weight: bfloat16 [2048, 1536], P('vocab', 'docs'), may hold values from -0.125 to 0.125
- head_bias: float32 [1536], replicated, may hold values from -4 to 4
- factor: bfloat16 [1536, 1536], P('vocab', 'docs'), as said below
- noise_draw: bfloat16 [65536, 1536], P(('vocab', 'docs')), may hold values from -5 to 5
Outputs:
- sample: bfloat16 [65536, 1536], P(('vocab', 'docs'))
Inputs may be any that keep to these rules, and one draw needn't show every extreme that they name: `doc_owner`: each document names 4 different owners. The documents of one device name one owner in at most 2 slots, and on some device some owner is named in exactly 2 slots. `factor`: lower triangular; diagonal entries lie between 0.5 and 1.5.
All inputs are finite; a program needn't handle non-finite values.
Results may differ from a plain program's by a relative error of at most 0.0038.
Values may be sent and summed in bfloat16 or wider, within the bound.
No kernel may reach another device: no remote copies, remote signals or barrier semaphores. Data moves between devices by JAX's collectives and lax.ppermute only.
A program may use at most 128 MiB of HBM per device.

v0:
```python
import jax
import jax.numpy as jnp
from jax import lax
from jax.sharding import PartitionSpec as P


def local(
    counts,
    doc_owner,
    doc_sub,
    doc_len,
    first_weight,
    first_bias,
    head_weight,
    head_bias,
    factor,
    noise_draw,
):
    vocab_devices = lax.axis_size("vocab")
    docs_devices = lax.axis_size("docs")
    device_count = vocab_devices * docs_devices
    docs_here, slot_count, block_width = counts.shape
    hidden_width = first_weight.shape[1]
    per_owner = first_weight.shape[0] // block_width
    capacity = max(2, 2 * docs_here * slot_count // device_count)
    owner_flat = doc_owner.reshape(-1)
    onehot = (owner_flat[:, None] == jnp.arange(device_count, dtype=jnp.int32)[None, :]).astype(
        jnp.int32
    )
    position = jnp.sum(jnp.cumsum(onehot, axis=0) * onehot, axis=1) - 1
    slot_index = owner_flat * capacity + position
    flat_rows = counts.reshape(-1, block_width)
    send_rows = (
        jnp.zeros((device_count * capacity, block_width), counts.dtype)
        .at[slot_index]
        .set(flat_rows)
    )
    send_sub = (
        jnp.zeros((device_count * capacity,), jnp.bfloat16)
        .at[slot_index]
        .set(doc_sub.reshape(-1).astype(jnp.bfloat16))
    )
    send_rows = send_rows.reshape(vocab_devices, docs_devices, capacity, block_width)
    send_sub = send_sub.reshape(vocab_devices, docs_devices, capacity)
    got_rows, got_sub = (
        lax.all_to_all(
            lax.all_to_all(send_rows, "vocab", split_axis=0, concat_axis=0, tiled=True),
            "docs",
            split_axis=1,
            concat_axis=1,
            tiled=True,
        ),
        lax.all_to_all(
            lax.all_to_all(send_sub, "vocab", split_axis=0, concat_axis=0, tiled=True),
            "docs",
            split_axis=1,
            concat_axis=1,
            tiled=True,
        ),
    )
    got_rows = got_rows.reshape(-1, block_width)
    got_sub = got_sub.reshape(-1).astype(jnp.int32)
    select = (got_sub[:, None] == jnp.arange(per_owner, dtype=jnp.int32)[None, :]).astype(
        jnp.bfloat16
    )
    spread = (select[:, :, None] * got_rows[:, None, :]).reshape(-1, per_owner * block_width)
    owner_terms = jnp.dot(spread, first_weight, preferred_element_type=jnp.float32).astype(
        jnp.bfloat16
    )
    owner_terms = owner_terms.reshape(vocab_devices, docs_devices, capacity, hidden_width)
    returned = lax.all_to_all(
        lax.all_to_all(owner_terms, "vocab", split_axis=0, concat_axis=0, tiled=True),
        "docs",
        split_axis=1,
        concat_axis=1,
        tiled=True,
    )
    returned = returned.reshape(-1, hidden_width)
    own_rows = returned[slot_index].reshape(docs_here, slot_count, hidden_width).astype(jnp.float32)
    summed = jnp.sum(own_rows, axis=1)
    length_scale = 128.0 * slot_count / doc_len.astype(jnp.float32)
    hidden = jax.nn.softplus(summed * length_scale[:, None] + first_bias).astype(jnp.bfloat16)
    panel_rows = lax.all_gather(head_weight, "docs", axis=1, tiled=True)
    location = jnp.dot(
        hidden,
        lax.all_gather(panel_rows, "vocab", axis=0, tiled=True),
        preferred_element_type=jnp.float32,
    )
    factor_panel = lax.all_gather(factor, "docs", axis=1, tiled=True)
    correlated = lax.dot_general(
        noise_draw,
        lax.all_gather(factor_panel, "vocab", axis=0, tiled=True),
        (((1,), (1,)), ((), ())),
        preferred_element_type=jnp.float32,
    )
    return (location + head_bias + correlated).astype(jnp.bfloat16)


def solution(mesh):
    return jax.shard_map(
        local,
        mesh=mesh,
        in_specs=(
            P(("vocab", "docs"), None, None),
            P(("vocab", "docs"), None),
            P(("vocab", "docs"), None),
            P(("vocab", "docs")),
            P(("vocab", "docs"), None),
            P(),
            P("vocab", "docs"),
            P(),
            P("vocab", "docs"),
            P(("vocab", "docs"), None),
        ),
        out_specs=P(("vocab", "docs"), None),
        check_vma=False,
    )
```

profile of v0, /device:TPU:1, one launch (start us, length us, event | category | flops | bytes accessed | tf_op | source)
XLA Modules:
  0.0 425.2 jit_solution(10619048773508162734)
XLA Ops:
  6.5 50.0 %all_gather.12 = bf16[128,1536]{0,1:T(8,128)(2,1)} all-gather(bf16[128,48]{0,1:T(8,128)(2,1)} %param.16), channel_id=1, replica_groups=mesh['vocab'=16,'docs'=32] {'docs'}, dimensions={1}, use_global_device_ids=true | all-gather | bytes 405504 | tf_op jit(solution)/shard_map/all_gather | solution.py:83
  59.3 3.8 scatter_custom_fusion
  64.1 18.7 %all-to-all-start = ((bf16[16,32,2]{1,2,0:T(2,128)(2,1)}), bf16[16,32,2]{1,2,0:T(2,128)(2,1)S(1)}, u32[]{:S(2)}, u32[]{:S(2)}) async-start(bf16[16,32,2]{1,2,0:T(2,128)(2,1)} %copy.63), calls=%async_computation | async-start | bytes 16384 | tf_op jit(solution)/shard_map/all_to_all | solution.py:54
  85.6 4.3 %all-to-all-done = bf16[16,32,2]{1,2,0:T(2,128)(2,1)S(1)} async-done(((bf16[16,32,2]{1,2,0:T(2,128)(2,1)}), bf16[16,32,2]{1,2,0:T(2,128)(2,1)S(1)}, u32[]{:S(2)}, u32[]{:S(2)}) %all-to-all-start) | async-done | bytes 2080 | tf_op jit(solution)/shard_map/all_to_all | solution.py:54
  90.0 3.9 all-to-all-start.2
  94.5 13.3 %all-to-all-done.2 = bf16[16,32,2,128]{3,2,1,0:T(2,128)(2,1)S(1)} async-done(((bf16[16,32,2,128]{3,2,1,0:T(2,128)(2,1)}), bf16[16,32,2,128]{3,2,1,0:T(2,128)(2,1)S(1)}, u32[]{:S(2)}, u32[]{:S(2)}) %all-to-all-start.2) | async-done | bytes 262176 | tf_op jit(solution)/shard_map/all_to_all | solution.py:47
  107.9 4.7 %all-to-all-start.1 = ((bf16[16,32,2]{0,2,1:T(2,128)(2,1)}), bf16[16,32,2]{0,2,1:T(2,128)(2,1)S(1)}, u32[]{:S(2)}, u32[]{:S(2)}) async-start(bf16[16,32,2]{0,2,1:T(2,128)(2,1)} %copy.64), calls=%async_computation.1 | async-start | bytes 32768 | tf_op jit(solution)/shard_map/all_to_all | solution.py:53
  113.5 7.7 %all-to-all-done.1 = bf16[16,32,2]{0,2,1:T(2,128)(2,1)S(1)} async-done(((bf16[16,32,2]{0,2,1:T(2,128)(2,1)}), bf16[16,32,2]{0,2,1:T(2,128)(2,1)S(1)}, u32[]{:S(2)}, u32[]{:S(2)}) %all-to-all-start.1) | async-done | bytes 2080 | tf_op jit(solution)/shard_map/all_to_all | solution.py:53
  121.2 4.0 all-to-all-start.3
  126.0 8.8 %all-to-all-done.3 = bf16[16,32,2,128]{3,2,0,1:T(2,128)(2,1)S(1)} async-done(((bf16[16,32,2,128]{3,2,0,1:T(2,128)(2,1)}), bf16[16,32,2,128]{3,2,0,1:T(2,128)(2,1)S(1)}, u32[]{:S(2)}, u32[]{:S(2)}) %all-to-all-start.3) | async-done | bytes 262176 | tf_op jit(solution)/shard_map/all_to_all | solution.py:46
  138.5 8.3 %convolution_convert_fusion = bf16[1024,2048]{1,0:T(8,128)(2,1)} fusion(bf16[1024,2048]{1,0:T(8,128)(2,1)} %param.14, bf16[128,8,8,128]{3,2,1,0:T(8,128)(2,1)S(1)} %bitcast.26), kind=kOutput, calls=%fused_computation.3 | convolution fusion | flops 4297064448 | bytes 10485760 | tf_op jit(solution)/shard_map/dot_general | solution.py:67
  146.8 7.6 %reshape.112 = bf16[16,32,2,2048]{3,2,1,0:T(2,128)(2,1)} reshape(bf16[1024,2048]{1,0:T(8,128)(2,1)} %convolution_convert_fusion) | data formatting | bytes 8388608 | tf_op jit(solution)/shard_map/reshape | solution.py:70
  154.4 8.1 %all-to-all-start.4 = ((bf16[16,32,2,2048]{3,2,1,0:T(2,128)(2,1)}), bf16[16,32,2,2048]{3,2,1,0:T(2,128)(2,1)}, u32[]{:S(2)}, u32[]{:S(2)}) async-start(bf16[16,32,2,2048]{3,2,1,0:T(2,128)(2,1)} %reshape.112), calls=%async_computation.4 | async-start | bytes 8388608 | tf_op jit(solution)/shard_map/all_to_all | solution.py:72
  162.5 40.7 %all_gather.14 = bf16[96,1536]{0,1:T(8,128)(2,1)S(1)} all-gather(bf16[96,48]{0,1:T(8,128)(2,1)S(1)} %copy-done.1), channel_id=1, replica_groups=mesh['vocab'=16,'docs'=32] {'docs'}, dimensions={1}, use_global_device_ids=true | all-gather | bytes 304128 | tf_op jit(solution)/shard_map/all_gather | solution.py:89
  204.2 65.5 %all-to-all-done.4 = bf16[16,32,2,2048]{3,2,1,0:T(2,128)(2,1)} async-done(((bf16[16,32,2,2048]{3,2,1,0:T(2,128)(2,1)}), bf16[16,32,2,2048]{3,2,1,0:T(2,128)(2,1)}, u32[]{:S(2)}, u32[]{:S(2)}) %all-to-all-start.4) | async-done | bytes 4194336 | tf_op jit(solution)/shard_map/all_to_all | solution.py:72
  269.7 8.8 %copy.69 = bf16[16,32,2,2048]{3,2,0,1:T(2,128)(2,1)} copy(bf16[16,32,2,2048]{3,2,1,0:T(2,128)(2,1)} %all-to-all-done.4) | data formatting | bytes 8388608 | tf_op jit(solution)/shard_map/all_to_all | solution.py:72
  278.5 5.2 %all-to-all-start.5 = ((bf16[16,32,2,2048]{3,2,0,1:T(2,128)(2,1)}), bf16[16,32,2,2048]{3,2,0,1:T(2,128)(2,1)}, u32[]{:S(2)}, u32[]{:S(2)}) async-start(bf16[16,32,2,2048]{3,2,0,1:T(2,128)(2,1)} %copy.69), calls=%async_computation.5 | async-start | bytes 8388608 | tf_op jit(solution)/shard_map/all_to_all | solution.py:71
  283.8 94.4 %all-to-all-done.5 = bf16[16,32,2,2048]{3,2,0,1:T(2,128)(2,1)} async-done(((bf16[16,32,2,2048]{3,2,0,1:T(2,128)(2,1)}), bf16[16,32,2,2048]{3,2,0,1:T(2,128)(2,1)}, u32[]{:S(2)}, u32[]{:S(2)}) %all-to-all-start.5) | async-done | bytes 4194336 | tf_op jit(solution)/shard_map/all_to_all | solution.py:71
  378.2 8.0 %copy.70 = bf16[16,32,2,2048]{3,2,1,0:T(2,128)(2,1)} copy(bf16[16,32,2,2048]{3,2,0,1:T(2,128)(2,1)} %all-to-all-done.5) | data formatting | bytes 8388608 | tf_op jit(solution)/shard_map/all_to_all | solution.py:71
  386.2 7.2 %reshape.113 = bf16[1024,2048]{1,0:T(8,128)(2,1)} reshape(bf16[16,32,2,2048]{3,2,1,0:T(2,128)(2,1)} %copy.70) | data formatting | bytes 8388608 | tf_op jit(solution)/shard_map/reshape | solution.py:78
  393.4 7.1 %gather_fusion = bf16[512,2048]{1,0:T(8,128)(2,1)S(1)} fusion(bf16[1024,2048]{1,0:T(8,128)(2,1)} %reshape.113, s32[1024]{0:T(1024)S(1)} %pad_clamp_fusion), kind=kCustom, calls=%fused_computation | custom fusion | bytes 4196352 | tf_op jit(solution)/shard_map/gather | solution.py:79
  403.6 4.8 %reduce_sum.19 = f32[128,2048]{1,0:T(8,128)S(1)} reduce(f32[128,4,2048]{2,1,0:T(4,128)} %reshape.115, f32[]{:T(128)} %constant.6.clone.1), dimensions={1}, to_apply=%region_5.6 | reduce | flops 786432 | bytes 5242884 | tf_op jit(solution)/shard_map/reduce_sum | solution.py:80
  408.5 5.1 %convolution_add_fusion.1 = f32[128,1536]{1,0:T(8,128)S(1)} fusion(bf16[2048,1536]{0,1:T(8,128)(2,1)} %all-gather.3.cloned.1.call-done, f32[128,2048]{1,0:T(8,128)S(1)} %reduce_sum.19, f32[2048]{0:T(1024)S(1)} %copy-done.4, f32[128]{0:T(128)S(1)} %convert_divide_fusion, f32[1536]{0:T(1024)S(1)} %copy-done.5), kind=kOutput, calls=%fused_computation.6 | convolution fusion | flops 807862272 | bytes 8141312 | tf_op jit(solution)/shard_map/dot_general | solution.py:84
  413.7 4.7 %fusion = bf16[128,1536]{1,0:T(8,128)(2,1)} fusion(f32[128,1536]{1,0:T(8,128)S(1)} %convolution_add_fusion.1, bf16[128,1536]{1,0:T(8,128)(2,1)S(1)} %copy-done, bf16[1536,1536]{1,0:T(8,128)(2,1)} %all-gather.5.cloned.1.call-done), kind=kOutput, calls=%fused_computation.7 | convolution fusion | flops 604372992 | bytes 6291456 | tf_op jit(solution)/shard_map/dot_general | solution.py:90
  (56 shorter events, 16.5 us)
Async XLA Ops:
  6.5 407.1 %copy-start = (bf16[128,1536]{1,0:T(8,128)(2,1)S(1)}, bf16[128,1536]{1,0:T(8,128)(2,1)}, u32[]{:S(2)}) copy-start(bf16[128,1536]{1,0:T(8,128)(2,1)} %param.19) | copy-start | bytes 1179652
  6.5 52.0 %copy-start.2 = (s32[128,4]{0,1:T(4,128)S(1)}, s32[128,4]{0,1:T(4,128)}, u32[]{:S(2)}) copy-start(s32[128,4]{0,1:T(4,128)} %param.11) | copy-start | bytes 6148
  6.5 52.2 %copy-start.3 = (s32[128,4]{0,1:T(4,128)S(1)}, s32[128,4]{0,1:T(4,128)}, u32[]{:S(2)}) copy-start(s32[128,4]{0,1:T(4,128)} %param.12) | copy-start | bytes 6148
  6.5 402.0 %all-gather.3.cloned.1.call-start = ((), (), s32[]{:S(2)}) async-start(), calls=%async_computation.6 | async-start | bytes 6684672 | tf_op jit(solution)/shard_map/all_gather | solution.py:86
  64.1 25.8 %all-to-all-start = ((bf16[16,32,2]{1,2,0:T(2,128)(2,1)}), bf16[16,32,2]{1,2,0:T(2,128)(2,1)S(1)}, u32[]{:S(2)}, u32[]{:S(2)}) async-start(bf16[16,32,2]{1,2,0:T(2,128)(2,1)} %copy.63), calls=%async_computation | async-start | bytes 16384 | tf_op jit(solution)/shard_map/all_to_all | solution.py:54
  90.0 17.9 %all-to-all-start.2 = ((bf16[16,32,2,128]{3,2,1,0:T(2,128)(2,1)}), bf16[16,32,2,128]{3,2,1,0:T(2,128)(2,1)S(1)}, u32[]{:S(2)}, u32[]{:S(2)}) async-start(bf16[16,32,2,128]{3,2,1,0:T(2,128)(2,1)} %bitcast.6), calls=%async_computation.2 | async-start | bytes 524288 | tf_op jit(solution)/shard_map/all_to_all | solution.py:47
  107.9 13.3 %all-to-all-start.1 = ((bf16[16,32,2]{0,2,1:T(2,128)(2,1)}), bf16[16,32,2]{0,2,1:T(2,128)(2,1)S(1)}, u32[]{:S(2)}, u32[]{:S(2)}) async-start(bf16[16,32,2]{0,2,1:T(2,128)(2,1)} %copy.64), calls=%async_computation.1 | async-start | bytes 32768 | tf_op jit(solution)/shard_map/all_to_all | solution.py:53
  121.2 13.5 %all-to-all-start.3 = ((bf16[16,32,2,128]{3,2,0,1:T(2,128)(2,1)}), bf16[16,32,2,128]{3,2,0,1:T(2,128)(2,1)S(1)}, u32[]{:S(2)}, u32[]{:S(2)}) async-start(bf16[16,32,2,128]{3,2,0,1:T(2,128)(2,1)} %copy.67), calls=%async_computation.3 | async-start | bytes 524288 | tf_op jit(solution)/shard_map/all_to_all | solution.py:46
  154.4 8.1 %copy-start.1 = (bf16[96,48]{0,1:T(8,128)(2,1)S(1)}, bf16[96,48]{0,1:T(8,128)(2,1)}, u32[]{:S(2)}) copy-start(bf16[96,48]{0,1:T(8,128)(2,1)} %param.18) | copy-start | bytes 27652
  154.4 115.3 %all-to-all-start.4 = ((bf16[16,32,2,2048]{3,2,1,0:T(2,128)(2,1)}), bf16[16,32,2,2048]{3,2,1,0:T(2,128)(2,1)}, u32[]{:S(2)}, u32[]{:S(2)}) async-start(bf16[16,32,2,2048]{3,2,1,0:T(2,128)(2,1)} %reshape.112), calls=%async_computation.4 | async-start | bytes 8388608 | tf_op jit(solution)/shard_map/all_to_all | solution.py:72
  162.5 251.2 %all-gather.5.cloned.1.call-start = ((), (), s32[]{:S(2)}) async-start(), calls=%async_computation.7 | async-start | bytes 5013504 | tf_op jit(solution)/shard_map/all_gather | solution.py:92
  278.5 5.2 %copy-start.6 = (s32[128]{0:T(128)S(1)}, s32[128]{0:T(128)}, u32[]{:S(2)}) copy-start(s32[128]{0:T(128)} %param.13) | copy-start | bytes 1540
  278.5 99.7 %all-to-all-start.5 = ((bf16[16,32,2,2048]{3,2,0,1:T(2,128)(2,1)}), bf16[16,32,2,2048]{3,2,0,1:T(2,128)(2,1)}, u32[]{:S(2)}, u32[]{:S(2)}) async-start(bf16[16,32,2,2048]{3,2,0,1:T(2,128)(2,1)} %copy.69), calls=%async_computation.5 | async-start | bytes 8388608 | tf_op jit(solution)/shard_map/all_to_all | solution.py:71
  403.6 4.9 %copy-start.4 = (f32[2048]{0:T(1024)S(1)}, f32[2048]{0:T(1024)}, u32[]{:S(2)}) copy-start(f32[2048]{0:T(1024)} %param.15) | copy-start | bytes 24580
  403.6 4.9 %copy-start.5 = (f32[1536]{0:T(1024)S(1)}, f32[1536]{0:T(1024)}, u32[]{:S(2)}) copy-start(f32[1536]{0:T(1024)} %param.17) | copy-start | bytes 18436
Sparse Core Ops, SparseCore 0:
  56.7 72.7 all-gather.2
  204.3 78.6 all-gather.4
where the time goes:
time: 426 us; the launch traced here: 425 us
  waiting for transfers between devices  194 us (46%)
  blocking collectives  90.8 us (21%)
  local copies, waits for them, and re-layouts  54.5 us (13%)
  starting transfers between devices  44.7 us (10%)
  matrix products  18.1 us (4%)
  between operations  13.7 us (3%)
  other arithmetic  9.24 us (2%)
    all_to_all x1, waiting for transfers between devices, local(): lax.all_to_all(lax.all_to_all(owner_terms, 'vocab', split_axis=0, concat_...  94.4 us
    all_to_all x1, waiting for transfers between devices, local(): lax.all_to_all(owner_terms, 'vocab', split_axis=0, concat_axis=0, tiled=T...  65.5 us
    all_gather x1, blocking collectives, local(): panel_rows = lax.all_gather(head_weight, 'docs', axis=1, tiled=True)  50 us
    all_gather x1, blocking collectives, local(): factor_panel = lax.all_gather(factor, 'docs', axis=1, tiled=True)  40.7 us
    all_to_all x1, starting transfers between devices, local(): lax.all_to_all(send_sub, 'vocab', split_axis=0, concat_axis=0, tiled=True)  18.7 us
    all_to_all x1, waiting for transfers between devices, local(): lax.all_to_all(send_rows, 'vocab', split_axis=0, concat_axis=0, tiled=True)  13.3 us
    all_to_all x1, waiting for transfers between devices, local(): lax.all_to_all(lax.all_to_all(send_rows, 'vocab', split_axis=0, concat_ax...  8.81 us
    all_to_all x1, local copies, waits for them, and re-layouts, local(): lax.all_to_all(owner_terms, 'vocab', split_axis=0, concat_axis=0, tiled=T...  8.8 us
  transfers between devices with their start and end apart: 8, of which 6 were waited for; matrix products, arithmetic and copies ran while one was open for 18% of the time, Pallas kernels for 0%

commit v1 on v0

--- a/solution.py
+++ b/solution.py
@@ -2,6 +2,29 @@
 import jax.numpy as jnp
 from jax import lax
 from jax.sharding import PartitionSpec as P
+
+
+def answer_cells_on_mesh(mine):
+    rack = []
+    b = 0
+    width = jax.lax.axis_size("vocab")
+    while b < width:
+        rack.append((b, (b + 1) % width))
+        b += 1
+    nodes = []
+    b = 0
+    while b < width:
+        nodes.append((b, (b - 1) % width))
+        b += 1
+    r2, high = ([mine], [mine])
+    for _ in range(width // 2):
+        r2.append(jax.lax.ppermute(r2[-1], "vocab", rack))
+    ix = 0
+    while ix < (width - 1) // 2:
+        high.append(jax.lax.ppermute(high[-1], "vocab", nodes))
+        ix = ix + 1
+    tmp = jnp.concatenate([*r2[::-1], *high[1:]], 0)
+    return jnp.roll(tmp, (jax.lax.axis_index("vocab") - width // 2) * mine.shape[0], 0)
 
 
 def local(
@@ -81,11 +104,7 @@
     length_scale = 128.0 * slot_count / doc_len.astype(jnp.float32)
     hidden = jax.nn.softplus(summed * length_scale[:, None] + first_bias).astype(jnp.bfloat16)
     panel_rows = lax.all_gather(head_weight, "docs", axis=1, tiled=True)
-    location = jnp.dot(
-        hidden,
-        lax.all_gather(panel_rows, "vocab", axis=0, tiled=True),
-        preferred_element_type=jnp.float32,
-    )
+    location = jnp.dot(hidden, answer_cells_on_mesh(panel_rows), preferred_element_type=jnp.float32)
     factor_panel = lax.all_gather(factor, "docs", axis=1, tiled=True)
     correlated = lax.dot_general(
         noise_draw,

time: 426 us -> 466 us (1.094); the launches traced: 425 us -> 457 us
  waiting for transfers between devices: 194 us -> 132 us
  starting transfers between devices: 44.7 us -> 106 us
  local copies, waits for them, and re-layouts: 54.5 us -> 94.7 us
  blocking collectives: 90.8 us -> 81.4 us
    all_to_all x1, waiting for transfers between devices: 65.5 us -> 0.01 us  [local(): lax.all_to_all(owner_terms, 'vocab', split_axis=0, concat_axis=0, tiled=T...]
    ppermute x0 -> x15, starting transfers between devices: none -> 63 us  [the longest x7 40.9 us: answer_cells_on_mesh(): high.append(jax.lax.ppermute(high[-1], 'vocab', nodes))]
    ppermute x0 -> x15, waiting for transfers between devices: none -> 56.8 us  [the longest x8 52.6 us: answer_cells_on_mesh(): r2.append(jax.lax.ppermute(r2[-1], 'vocab', rack))]
    all_to_all x1, waiting for transfers between devices: 94.4 us -> 43.1 us  [local(): lax.all_to_all(lax.all_to_all(owner_terms, 'vocab', split_axis=0, concat_...]
    unnamed x16 -> x51, local copies, waits for them, and re-layouts: 0.82 us -> 39.3 us
    all_gather x1, blocking collectives: 50 us -> 40.7 us  [local(): panel_rows = lax.all_gather(head_weight, 'docs', axis=1, tiled=True)]
    all_to_all x1, starting transfers between devices: 18.7 us -> 10.1 us  [local(): lax.all_to_all(send_sub, 'vocab', split_axis=0, concat_axis=0, tiled=True)]
    all_to_all x1, starting transfers between devices: 4.7 us -> 11.3 us  [local(): lax.all_to_all(lax.all_to_all(send_sub, 'vocab', split_axis=0, concat_axi...]
  transfers between devices with their start and end apart: 8 -> 22, of which waited for: 6 -> 13; matrix products, arithmetic and copies ran while one was open for 18% -> 13% of each run, Pallas kernels for 0% -> 0%
where the time goes in v1:
time: 466 us; the launch traced here: 457 us
  waiting for transfers between devices  132 us (28%)
  starting transfers between devices  106 us (23%)
  local copies, waits for them, and re-layouts  94.7 us (20%)
  blocking collectives  81.4 us (17%)
  matrix products  18.1 us (4%)
  between operations  13.6 us (3%)
  other arithmetic  11.3 us (2%)
    ppermute x8, waiting for transfers between devices, answer_cells_on_mesh(): r2.append(jax.lax.ppermute(r2[-1], 'vocab', rack))  52.6 us
    all_to_all x1, waiting for transfers between devices, local(): lax.all_to_all(lax.all_to_all(owner_terms, 'vocab', split_axis=0, concat_...  43.1 us
    ppermute x7, starting transfers between devices, answer_cells_on_mesh(): high.append(jax.lax.ppermute(high[-1], 'vocab', nodes))  40.9 us
    all_gather x1, blocking collectives, local(): factor_panel = lax.all_gather(factor, 'docs', axis=1, tiled=True)  40.7 us
    all_gather x1, blocking collectives, local(): panel_rows = lax.all_gather(head_weight, 'docs', axis=1, tiled=True)  40.7 us
    unnamed x51, local copies, waits for them, and re-layouts  39.3 us
    ppermute x8, starting transfers between devices, answer_cells_on_mesh(): r2.append(jax.lax.ppermute(r2[-1], 'vocab', rack))  22.1 us
    all_to_all x1, starting transfers between devices, local(): lax.all_to_all(lax.all_to_all(send_sub, 'vocab', split_axis=0, concat_axi...  11.3 us
  transfers between devices with their start and end apart: 22, of which 13 were waited for; matrix products, arithmetic and copies ran while one was open for 13% of the time, Pallas kernels for 0%

profile of v1, /device:TPU:1, one launch (start us, length us, event | category | flops | bytes accessed | tf_op | source)
XLA Modules:
  0.0 456.5 jit_solution(10180993587252881399)
XLA Ops:
  15.4 10.1 %all-to-all-start = ((bf16[16,32,2]{1,2,0:T(2,128)(2,1)}), bf16[16,32,2]{1,2,0:T(2,128)(2,1)S(1)}, u32[]{:S(2)}, u32[]{:S(2)}) async-start(bf16[16,32,2]{1,2,0:T(2,128)(2,1)} %copy.63), calls=%async_computation | async-start | bytes 16384 | tf_op jit(solution)/shard_map/all_to_all | solution.py:77
  28.4 4.3 all-to-all-done
  37.3 11.2 %all-to-all-done.2 = bf16[16,32,2,128]{3,2,1,0:T(2,128)(2,1)S(1)} async-done(((bf16[16,32,2,128]{3,2,1,0:T(2,128)(2,1)}), bf16[16,32,2,128]{3,2,1,0:T(2,128)(2,1)S(1)}, u32[]{:S(2)}, u32[]{:S(2)}) %all-to-all-start.2) | async-done | bytes 262176 | tf_op jit(solution)/shard_map/all_to_all | solution.py:70
  48.5 11.3 %all-to-all-start.1 = ((bf16[16,32,2]{0,2,1:T(2,128)(2,1)}), bf16[16,32,2]{0,2,1:T(2,128)(2,1)S(1)}, u32[]{:S(2)}, u32[]{:S(2)}) async-start(bf16[16,32,2]{0,2,1:T(2,128)(2,1)} %copy.64), calls=%async_computation.1 | async-start | bytes 32768 | tf_op jit(solution)/shard_map/all_to_all | solution.py:76
  60.7 7.7 %all-to-all-done.1 = bf16[16,32,2]{0,2,1:T(2,128)(2,1)S(1)} async-done(((bf16[16,32,2]{0,2,1:T(2,128)(2,1)}), bf16[16,32,2]{0,2,1:T(2,128)(2,1)S(1)}, u32[]{:S(2)}, u32[]{:S(2)}) %all-to-all-start.1) | async-done | bytes 2080 | tf_op jit(solution)/shard_map/all_to_all | solution.py:76
  73.1 8.8 %all-to-all-done.3 = bf16[16,32,2,128]{3,2,0,1:T(2,128)(2,1)S(1)} async-done(((bf16[16,32,2,128]{3,2,0,1:T(2,128)(2,1)}), bf16[16,32,2,128]{3,2,0,1:T(2,128)(2,1)S(1)}, u32[]{:S(2)}, u32[]{:S(2)}) %all-to-all-start.3) | async-done | bytes 262176 | tf_op jit(solution)/shard_map/all_to_all | solution.py:69
  85.7 8.3 %convolution_convert_fusion = bf16[1024,2048]{1,0:T(8,128)(2,1)} fusion(bf16[1024,2048]{1,0:T(8,128)(2,1)} %param.14, bf16[128,8,8,128]{3,2,1,0:T(8,128)(2,1)S(1)} %bitcast.25), kind=kOutput, calls=%fused_computation.5 | convolution fusion | flops 4297064448 | bytes 10485760 | tf_op jit(solution)/shard_map/dot_general | solution.py:90
  94.0 7.6 %reshape.112 = bf16[16,32,2,2048]{3,2,1,0:T(2,128)(2,1)} reshape(bf16[1024,2048]{1,0:T(8,128)(2,1)} %convolution_convert_fusion) | data formatting | bytes 8388608 | tf_op jit(solution)/shard_map/reshape | solution.py:93
  101.7 7.9 %all-to-all-start.4 = ((bf16[16,32,2,2048]{3,2,1,0:T(2,128)(2,1)}), bf16[16,32,2,2048]{3,2,1,0:T(2,128)(2,1)}, u32[]{:S(2)}, u32[]{:S(2)}) async-start(bf16[16,32,2,2048]{3,2,1,0:T(2,128)(2,1)} %reshape.112), calls=%async_computation.4 | async-start | bytes 8388608 | tf_op jit(solution)/shard_map/all_to_all | solution.py:95
  109.6 40.7 %all_gather.9 = bf16[128,1536]{0,1:T(8,128)(2,1)S(1)} all-gather(bf16[128,48]{0,1:T(8,128)(2,1)S(1)} %copy-done.5), channel_id=1, replica_groups=mesh['vocab'=16,'docs'=32] {'docs'}, dimensions={1}, use_global_device_ids=true | all-gather | bytes 405504 | tf_op jit(solution)/shard_map/all_gather | solution.py:106
  150.3 8.9 %collective-permute-start = (bf16[128,1536]{0,1:T(8,128)(2,1)S(1)}, bf16[128,1536]{0,1:T(8,128)(2,1)S(1)}, u32[]{:S(2)}, u32[]{:S(2)}) collective-permute-start(bf16[128,1536]{0,1:T(8,128)(2,1)S(1)} %all_gather.9), channel_id=1, source_target_pairs={{0,32},{32,64},{64,96},{96,128},{128,160},{160,192},{192,224},{224... | collective-permute-start | bytes 1179656 | tf_op jit(solution)/shard_map/ppermute | solution.py:21
  159.3 45.4 %collective-permute-done = bf16[128,1536]{0,1:T(8,128)(2,1)S(1)} collective-permute-done((bf16[128,1536]{0,1:T(8,128)(2,1)S(1)}, bf16[128,1536]{0,1:T(8,128)(2,1)S(1)}, u32[]{:S(2)}, u32[]{:S(2)}) %collective-permute-start) | collective-permute-done | bytes 393248 | tf_op jit(solution)/shard_map/ppermute | solution.py:21
  228.7 40.7 %all_gather.10 = bf16[96,1536]{0,1:T(8,128)(2,1)} all-gather(bf16[96,48]{0,1:T(8,128)(2,1)S(1)} %copy-done.6), channel_id=1, replica_groups=mesh['vocab'=16,'docs'=32] {'docs'}, dimensions={1}, use_global_device_ids=true | all-gather | bytes 304128 | tf_op jit(solution)/shard_map/all_gather | solution.py:108
  271.4 16.1 %collective-permute-start.11 = (bf16[128,1536]{0,1:T(8,128)(2,1)S(1)}, bf16[128,1536]{0,1:T(8,128)(2,1)S(1)}, u32[]{:S(2)}, u32[]{:S(2)}) collective-permute-start(bf16[128,1536]{0,1:T(8,128)(2,1)S(1)} %collective-permute-done.10), channel_id=1, source_target_pairs={{0,480},{32,0},{64,32},{96,64},{128,96},{160,128},{192,160},{224,1... | collective-permute-start | bytes 1179656 | tf_op jit(solution)/shard_map/ppermute | solution.py:24
  296.9 10.5 %collective-permute-start.13 = (bf16[128,1536]{0,1:T(8,128)(2,1)}, bf16[128,1536]{0,1:T(8,128)(2,1)}, u32[]{:S(2)}, u32[]{:S(2)}) collective-permute-start(bf16[128,1536]{0,1:T(8,128)(2,1)} %collective-permute-done.12), channel_id=1, source_target_pairs={{0,480},{32,0},{64,32},{96,64},{128,96},{160,128},{192,160},{224,1... | collective-permute-start | bytes 1179656 | tf_op jit(solution)/shard_map/ppermute | solution.py:24
  309.3 8.8 %copy.69 = bf16[16,32,2,2048]{3,2,0,1:T(2,128)(2,1)} copy(bf16[16,32,2,2048]{3,2,1,0:T(2,128)(2,1)} %all-to-all-done.4) | data formatting | bytes 8388608 | tf_op jit(solution)/shard_map/all_to_all | solution.py:95
  318.1 5.1 %all-to-all-start.5 = ((bf16[16,32,2,2048]{3,2,0,1:T(2,128)(2,1)}), bf16[16,32,2,2048]{3,2,0,1:T(2,128)(2,1)}, u32[]{:S(2)}, u32[]{:S(2)}) async-start(bf16[16,32,2,2048]{3,2,0,1:T(2,128)(2,1)} %copy.69), calls=%async_computation.5 | async-start | bytes 8388608 | tf_op jit(solution)/shard_map/all_to_all | solution.py:94
  323.9 4.2 collective-permute-start.14
  370.5 43.1 %all-to-all-done.5 = bf16[16,32,2,2048]{3,2,0,1:T(2,128)(2,1)} async-done(((bf16[16,32,2,2048]{3,2,0,1:T(2,128)(2,1)}), bf16[16,32,2,2048]{3,2,0,1:T(2,128)(2,1)}, u32[]{:S(2)}, u32[]{:S(2)}) %all-to-all-start.5) | async-done | bytes 4194336 | tf_op jit(solution)/shard_map/all_to_all | solution.py:94
  413.6 8.0 %copy.70 = bf16[16,32,2,2048]{3,2,1,0:T(2,128)(2,1)} copy(bf16[16,32,2,2048]{3,2,0,1:T(2,128)(2,1)} %all-to-all-done.5) | data formatting | bytes 8388608 | tf_op jit(solution)/shard_map/all_to_all | solution.py:94
  421.6 7.2 %reshape.113 = bf16[1024,2048]{1,0:T(8,128)(2,1)} reshape(bf16[16,32,2,2048]{3,2,1,0:T(2,128)(2,1)} %copy.70) | data formatting | bytes 8388608 | tf_op jit(solution)/shard_map/reshape | solution.py:101
  428.7 7.2 %gather_fusion = bf16[512,2048]{1,0:T(8,128)(2,1)S(1)} fusion(bf16[1024,2048]{1,0:T(8,128)(2,1)} %reshape.113, s32[1024]{0:T(1024)S(1)} %pad_clamp_fusion), kind=kCustom, calls=%fused_computation | custom fusion | bytes 4196352 | tf_op jit(solution)/shard_map/gather | solution.py:102
  439.0 4.8 %reduce_sum.19 = f32[128,2048]{1,0:T(8,128)S(1)} reduce(f32[128,4,2048]{2,1,0:T(4,128)} %reshape.115, f32[]{:T(128)} %constant.46.clone.1), dimensions={1}, to_apply=%region_5.6 | reduce | flops 786432 | bytes 5242884 | tf_op jit(solution)/shard_map/reduce_sum | solution.py:103
  443.8 5.9 %fusion.8 = bf16[128,1536]{1,0:T(8,128)(2,1)} fusion(f32[128,1536]{1,0:T(8,128)S(1)} %fusion.29, bf16[4096,1536]{0,1:T(8,128)(2,1)} %constant_dynamic-update-slice_fusion, s32[]{:T(128)S(6)} %select_n.32, f32[128,2048]{1,0:T(8,128)S(1)} %reduce_sum.19, f32[2048]{0:T(1024)S(1)} %copy-done.7, f32[128]{0:T(128)S(1)} %convert_divide_fusion, f32[1536]{0:T(1024)S(1)} %copy-done.8), kind=kOutput, calls=%fused_computation.9 | convolution fusion | flops 808255488 | bytes 8534532 | tf_op jit(solution)/shard_map/dot_general | solution.py:107
  (119 shorter events, 109.1 us)
Async XLA Ops:
  6.5 360.0 %copy-start = (bf16[128,1536]{1,0:T(8,128)(2,1)S(1)}, bf16[128,1536]{1,0:T(8,128)(2,1)}, u32[]{:S(2)}) copy-start(bf16[128,1536]{1,0:T(8,128)(2,1)} %param.19) | copy-start | bytes 1179652
  15.4 17.2 %all-to-all-start = ((bf16[16,32,2]{1,2,0:T(2,128)(2,1)}), bf16[16,32,2]{1,2,0:T(2,128)(2,1)S(1)}, u32[]{:S(2)}, u32[]{:S(2)}) async-start(bf16[16,32,2]{1,2,0:T(2,128)(2,1)} %copy.63), calls=%async_computation | async-start | bytes 16384 | tf_op jit(solution)/shard_map/all_to_all | solution.py:77
  32.7 15.8 %all-to-all-start.2 = ((bf16[16,32,2,128]{3,2,1,0:T(2,128)(2,1)}), bf16[16,32,2,128]{3,2,1,0:T(2,128)(2,1)S(1)}, u32[]{:S(2)}, u32[]{:S(2)}) async-start(bf16[16,32,2,128]{3,2,1,0:T(2,128)(2,1)} %bitcast.6), calls=%async_computation.2 | async-start | bytes 524288 | tf_op jit(solution)/shard_map/all_to_all | solution.py:70
  48.5 19.9 %all-to-all-start.1 = ((bf16[16,32,2]{0,2,1:T(2,128)(2,1)}), bf16[16,32,2]{0,2,1:T(2,128)(2,1)S(1)}, u32[]{:S(2)}, u32[]{:S(2)}) async-start(bf16[16,32,2]{0,2,1:T(2,128)(2,1)} %copy.64), calls=%async_computation.1 | async-start | bytes 32768 | tf_op jit(solution)/shard_map/all_to_all | solution.py:76
  68.4 13.6 %all-to-all-start.3 = ((bf16[16,32,2,128]{3,2,0,1:T(2,128)(2,1)}), bf16[16,32,2,128]{3,2,0,1:T(2,128)(2,1)S(1)}, u32[]{:S(2)}, u32[]{:S(2)}) async-start(bf16[16,32,2,128]{3,2,0,1:T(2,128)(2,1)} %copy.67), calls=%async_computation.3 | async-start | bytes 524288 | tf_op jit(solution)/shard_map/all_to_all | solution.py:69
  94.0 134.7 %copy-start.6 = (bf16[96,48]{0,1:T(8,128)(2,1)S(1)}, bf16[96,48]{0,1:T(8,128)(2,1)}, u32[]{:S(2)}) copy-start(bf16[96,48]{0,1:T(8,128)(2,1)} %param.18) | copy-start | bytes 27652
  101.7 207.6 %all-to-all-start.4 = ((bf16[16,32,2,2048]{3,2,1,0:T(2,128)(2,1)}), bf16[16,32,2,2048]{3,2,1,0:T(2,128)(2,1)}, u32[]{:S(2)}, u32[]{:S(2)}) async-start(bf16[16,32,2,2048]{3,2,1,0:T(2,128)(2,1)} %reshape.112), calls=%async_computation.4 | async-start | bytes 8388608 | tf_op jit(solution)/shard_map/all_to_all | solution.py:95
  109.6 257.0 %all-gather.2.cloned.1.call-start = ((), (), s32[]{:S(2)}) async-start(), calls=%async_computation.6 | async-start | bytes 5013504 | tf_op jit(solution)/shard_map/all_gather | solution.py:111
  150.3 54.3 %collective-permute-start = (bf16[128,1536]{0,1:T(8,128)(2,1)S(1)}, bf16[128,1536]{0,1:T(8,128)(2,1)S(1)}, u32[]{:S(2)}, u32[]{:S(2)}) collective-permute-start(bf16[128,1536]{0,1:T(8,128)(2,1)S(1)} %all_gather.9), channel_id=1, source_target_pairs={{0,32},{32,64},{64,96},{96,128},{128,160},{160,192},{192,224},{224... | collective-permute-start | bytes 1179656 | tf_op jit(solution)/shard_map/ppermute | solution.py:21
  204.6 7.2 %collective-permute-start.1 = (bf16[128,1536]{0,1:T(8,128)(2,1)S(1)}, bf16[128,1536]{0,1:T(8,128)(2,1)S(1)}, u32[]{:S(2)}, u32[]{:S(2)}) collective-permute-start(bf16[128,1536]{0,1:T(8,128)(2,1)S(1)} %collective-permute-done), channel_id=1, source_target_pairs={{0,32},{32,64},{64,96},{96,128},{128,160},{160,192},{192,224},{224... | collective-permute-start | bytes 1179656 | tf_op jit(solution)/shard_map/ppermute | solution.py:21
  207.1 7.5 %collective-permute-start.8 = (bf16[128,1536]{0,1:T(8,128)(2,1)S(1)}, bf16[128,1536]{0,1:T(8,128)(2,1)S(1)}, u32[]{:S(2)}, u32[]{:S(2)}) collective-permute-start(bf16[128,1536]{0,1:T(8,128)(2,1)S(1)} %all_gather.9), channel_id=1, source_target_pairs={{0,480},{32,0},{64,32},{96,64},{128,96},{160,128},{192,160},{224,1... | collective-permute-start | bytes 1179656 | tf_op jit(solution)/shard_map/ppermute | solution.py:24
  211.8 7.2 %collective-permute-start.2 = (bf16[128,1536]{0,1:T(8,128)(2,1)S(1)}, bf16[128,1536]{0,1:T(8,128)(2,1)S(1)}, u32[]{:S(2)}, u32[]{:S(2)}) collective-permute-start(bf16[128,1536]{0,1:T(8,128)(2,1)S(1)} %collective-permute-done.1), channel_id=1, source_target_pairs={{0,32},{32,64},{64,96},{96,128},{128,160},{160,192},{192,224},{224... | collective-permute-start | bytes 1179656 | tf_op jit(solution)/shard_map/ppermute | solution.py:21
  214.6 7.5 %collective-permute-start.9 = (bf16[128,1536]{0,1:T(8,128)(2,1)S(1)}, bf16[128,1536]{0,1:T(8,128)(2,1)S(1)}, u32[]{:S(2)}, u32[]{:S(2)}) collective-permute-start(bf16[128,1536]{0,1:T(8,128)(2,1)S(1)} %collective-permute-done.8), channel_id=1, source_target_pairs={{0,480},{32,0},{64,32},{96,64},{128,96},{160,128},{192,160},{224,1... | collective-permute-start | bytes 1179656 | tf_op jit(solution)/shard_map/ppermute | solution.py:24
  219.0 7.2 %collective-permute-start.3 = (bf16[128,1536]{0,1:T(8,128)(2,1)S(1)}, bf16[128,1536]{0,1:T(8,128)(2,1)S(1)}, u32[]{:S(2)}, u32[]{:S(2)}) collective-permute-start(bf16[128,1536]{0,1:T(8,128)(2,1)S(1)} %collective-permute-done.2), channel_id=1, source_target_pairs={{0,32},{32,64},{64,96},{96,128},{128,160},{160,192},{192,224},{224... | collective-permute-start | bytes 1179656 | tf_op jit(solution)/shard_map/ppermute | solution.py:21
  222.1 49.2 %collective-permute-start.10 = (bf16[128,1536]{0,1:T(8,128)(2,1)S(1)}, bf16[128,1536]{0,1:T(8,128)(2,1)S(1)}, u32[]{:S(2)}, u32[]{:S(2)}) collective-permute-start(bf16[128,1536]{0,1:T(8,128)(2,1)S(1)} %collective-permute-done.9), channel_id=1, source_target_pairs={{0,480},{32,0},{64,32},{96,64},{128,96},{160,128},{192,160},{224,1... | collective-permute-start | bytes 1179656 | tf_op jit(solution)/shard_map/ppermute | solution.py:24
  226.3 61.2 %collective-permute-start.4 = (bf16[128,1536]{0,1:T(8,128)(2,1)S(1)}, bf16[128,1536]{0,1:T(8,128)(2,1)}, u32[]{:S(2)}, u32[]{:S(2)}) collective-permute-start(bf16[128,1536]{0,1:T(8,128)(2,1)S(1)} %collective-permute-done.3), channel_id=1, source_target_pairs={{0,32},{32,64},{64,96},{96,128},{128,160},{160,192},{192,224},{224... | collective-permute-start | bytes 1179656 | tf_op jit(solution)/shard_map/ppermute | solution.py:21
  271.4 17.4 %collective-permute-start.11 = (bf16[128,1536]{0,1:T(8,128)(2,1)S(1)}, bf16[128,1536]{0,1:T(8,128)(2,1)S(1)}, u32[]{:S(2)}, u32[]{:S(2)}) collective-permute-start(bf16[128,1536]{0,1:T(8,128)(2,1)S(1)} %collective-permute-done.10), channel_id=1, source_target_pairs={{0,480},{32,0},{64,32},{96,64},{128,96},{160,128},{192,160},{224,1... | collective-permute-start | bytes 1179656 | tf_op jit(solution)/shard_map/ppermute | solution.py:24
  287.5 6.0 %collective-permute-start.5 = (bf16[128,1536]{0,1:T(8,128)(2,1)}, bf16[128,1536]{0,1:T(8,128)(2,1)S(1)}, u32[]{:S(2)}, u32[]{:S(2)}) collective-permute-start(bf16[128,1536]{0,1:T(8,128)(2,1)} %collective-permute-done.4), channel_id=1, source_target_pairs={{0,32},{32,64},{64,96},{96,128},{128,160},{160,192},{192,224},{224... | collective-permute-start | bytes 1179656 | tf_op jit(solution)/shard_map/ppermute | solution.py:21
  289.5 7.3 %collective-permute-start.12 = (bf16[128,1536]{0,1:T(8,128)(2,1)S(1)}, bf16[128,1536]{0,1:T(8,128)(2,1)}, u32[]{:S(2)}, u32[]{:S(2)}) collective-permute-start(bf16[128,1536]{0,1:T(8,128)(2,1)S(1)} %collective-permute-done.11), channel_id=1, source_target_pairs={{0,480},{32,0},{64,32},{96,64},{128,96},{160,128},{192,160},{224,1... | collective-permute-start | bytes 1179656 | tf_op jit(solution)/shard_map/ppermute | solution.py:24
  293.5 13.9 %collective-permute-start.6 = (bf16[128,1536]{0,1:T(8,128)(2,1)S(1)}, bf16[128,1536]{0,1:T(8,128)(2,1)}, u32[]{:S(2)}, u32[]{:S(2)}) collective-permute-start(bf16[128,1536]{0,1:T(8,128)(2,1)S(1)} %collective-permute-done.5), channel_id=1, source_target_pairs={{0,32},{32,64},{64,96},{96,128},{128,160},{160,192},{192,224},{224... | collective-permute-start | bytes 1179656 | tf_op jit(solution)/shard_map/ppermute | solution.py:21
  296.9 27.0 %collective-permute-start.13 = (bf16[128,1536]{0,1:T(8,128)(2,1)}, bf16[128,1536]{0,1:T(8,128)(2,1)}, u32[]{:S(2)}, u32[]{:S(2)}) collective-permute-start(bf16[128,1536]{0,1:T(8,128)(2,1)} %collective-permute-done.12), channel_id=1, source_target_pairs={{0,480},{32,0},{64,32},{96,64},{128,96},{160,128},{192,160},{224,1... | collective-permute-start | bytes 1179656 | tf_op jit(solution)/shard_map/ppermute | solution.py:24
  307.4 20.7 %collective-permute-start.7 = (bf16[128,1536]{0,1:T(8,128)(2,1)}, bf16[128,1536]{0,1:T(8,128)(2,1)}, u32[]{:S(2)}, u32[]{:S(2)}) collective-permute-start(bf16[128,1536]{0,1:T(8,128)(2,1)} %collective-permute-done.6), channel_id=1, source_target_pairs={{0,32},{32,64},{64,96},{96,128},{128,160},{160,192},{192,224},{224... | collective-permute-start | bytes 1179656 | tf_op jit(solution)/shard_map/ppermute | solution.py:21
  318.1 95.5 %all-to-all-start.5 = ((bf16[16,32,2,2048]{3,2,0,1:T(2,128)(2,1)}), bf16[16,32,2,2048]{3,2,0,1:T(2,128)(2,1)}, u32[]{:S(2)}, u32[]{:S(2)}) async-start(bf16[16,32,2,2048]{3,2,0,1:T(2,128)(2,1)} %copy.69), calls=%async_computation.5 | async-start | bytes 8388608 | tf_op jit(solution)/shard_map/all_to_all | solution.py:94
  323.9 23.6 %collective-permute-start.14 = (bf16[128,1536]{0,1:T(8,128)(2,1)}, bf16[128,1536]{0,1:T(8,128)(2,1)S(1)}, u32[]{:S(2)}, u32[]{:S(2)}) collective-permute-start(bf16[128,1536]{0,1:T(8,128)(2,1)} %collective-permute-done.13), channel_id=1, source_target_pairs={{0,480},{32,0},{64,32},{96,64},{128,96},{160,128},{192,160},{224,1... | collective-permute-start | bytes 1179656 | tf_op jit(solution)/shard_map/ppermute | solution.py:24
  (7 other events, 115.4 us)
Sparse Core Ops, SparseCore 0:
  271.5 61.1 all-gather.1
